TPU v7x, 32 devices: a whole 2x2x4 slice. The times are simulated.
32 devices in a mesh: wide: 16 (over z, y, core), narrow: 2 (over x).
Axes of the slice: x: 2, y: 2, z: 4, core: 2. Of those that a mesh axis runs over, the one named last changes fastest.
Arguments:
- hidden_in: bfloat16 [4096, 2048], P('wide', 'narrow'), may hold values from -64 to 64
- cache_lengths: int32 [32], P('wide'), may hold values from 1 to 1023, as said below
- cache_offsets: int32 [32], P('wide'), may hold values from 0 to 16383, as said below
- cache_kv: bfloat16 [2, 2, 16384, 2048], P(None, None, 'wide', 'narrow'), may hold values from -16 to 16
- w_qkv: bfloat16 [2048, 3, 2048], P('wide', None, 'narrow'), may hold values from -0.125 to 0.125
- qkv_bias: bfloat16 [3, 2048], P(None, 'narrow'), may hold values from -40 to 40
- w_out: bfloat16 [2048, 2048], P('wide', 'narrow'), may hold values from -0.125 to 0.125
- out_bias: bfloat16 [2048], P('narrow'), may hold values from -3 to 3
- norm_gain: bfloat16 [2048], P('narrow'), may hold values from 0.2 to 5
- norm_shift: bfloat16 [2048], P('narrow'), may hold values from -3 to 3
Outputs:
- hidden_out: bfloat16 [4096, 2048], P('wide', 'narrow')
- new_cache: bfloat16 [2, 2, 4096, 2048], P(None, None, 'wide', 'narrow')
Inputs may be any that keep to these rules, and one draw needn't show every extreme that they name: `cache_lengths`: the cached lengths of the 2 requests r with the same r // 2 sum to at most 1024; for some such group exactly 1024, and in it one request has 1023 rows. Request r's cache is rows cache_offsets[r] to cache_offsets[r] + cache_lengths[r] - 1 of the packed cache, all within rows (r // 2) * 1024 to (r // 2 + 1) * 1024 - 1; the row ranges of different requests are disjoint.
All inputs are finite; a program needn't handle non-finite values.
Results may differ from a plain program's by a relative error of at most 0.02.
Values may be sent and summed in bfloat16 or wider, within the bound.
A program may use at most 128 MiB of HBM per device.

v0:
```python
import math

import jax
import jax.numpy as jnp
from jax import lax
from jax.sharding import PartitionSpec as P

HEAD = 128
SPAN = 128
LAYERS = 2


EPSILON = 1e-05
NEGATIVE = -1e30


def add_rows(shard_piece, operand):
    piece_rows = shard_piece.shape[0]
    return jnp.dot(operand, shard_piece.reshape(piece_rows, -1), preferred_element_type=jnp.float32)


def norm_slice(summed, norm_gain, norm_shift, full_width):
    values = summed.astype(jnp.float32)
    row_means = lax.psum(jnp.sum(values, axis=1), "narrow") / full_width
    centered = values - row_means[:, None]
    row_spread = lax.psum(jnp.sum(centered * centered, axis=1), "narrow") / full_width
    scaled = centered * lax.rsqrt(row_spread[:, None] + EPSILON)
    return (scaled * norm_gain.astype(jnp.float32) + norm_shift.astype(jnp.float32)).astype(
        jnp.bfloat16
    )


def attend(queries, keys_new, values_new, keys_cache, values_cache, live_cache, live_new):
    scale_factor = 1.0 / math.sqrt(queries.shape[2])
    scores_cache = (
        jnp.einsum("qhd,khd->hqk", queries, keys_cache, preferred_element_type=jnp.float32)
        * scale_factor
    )
    scores_new = (
        jnp.einsum("qhd,khd->hqk", queries, keys_new, preferred_element_type=jnp.float32)
        * scale_factor
    )
    masked_cache = jnp.where(live_cache[None], scores_cache, NEGATIVE)
    masked_new = jnp.where(live_new[None], scores_new, NEGATIVE)
    top_score = jnp.maximum(jnp.max(masked_cache, axis=2), jnp.max(masked_new, axis=2))[:, :, None]
    weights_cache = jnp.where(live_cache[None], jnp.exp(masked_cache - top_score), 0.0)
    weights_new = jnp.where(live_new[None], jnp.exp(masked_new - top_score), 0.0)
    totals = jnp.sum(weights_cache, axis=2, keepdims=True) + jnp.sum(
        weights_new, axis=2, keepdims=True
    )
    probs_cache = (weights_cache / totals).astype(jnp.bfloat16)
    probs_new = (weights_new / totals).astype(jnp.bfloat16)
    combined = jnp.einsum(
        "hqk,khd->qhd", probs_cache, values_cache, preferred_element_type=jnp.float32
    )
    combined = combined + jnp.einsum(
        "hqk,khd->qhd", probs_new, values_new, preferred_element_type=jnp.float32
    )
    return combined.astype(jnp.bfloat16).reshape(queries.shape[0], -1)


def shards(
    hidden_in,
    cache_lengths,
    cache_offsets,
    cache_kv,
    w_qkv,
    qkv_bias,
    w_out,
    out_bias,
    norm_gain,
    norm_shift,
):
    row_count, local_width = hidden_in.shape
    full_width = local_width * lax.axis_size("narrow")
    local_heads = local_width // HEAD
    cache_count = cache_kv.shape[2]
    requests_here = cache_lengths.shape[0]
    block_start = lax.axis_index("wide") * cache_count
    rows_global = block_start + jnp.arange(cache_count, dtype=jnp.int32)
    row_start = jnp.broadcast_to(cache_offsets[:, None], (requests_here, SPAN)).reshape(-1)
    row_stop = row_start + jnp.broadcast_to(cache_lengths[:, None], (requests_here, SPAN)).reshape(
        -1
    )
    live_cache = (rows_global[None, :] >= row_start[:, None]) & (
        rows_global[None, :] < row_stop[:, None]
    )
    owner_index = jnp.arange(row_count, dtype=jnp.int32) // SPAN
    position = jnp.arange(row_count, dtype=jnp.int32) % SPAN
    live_new = (owner_index[:, None] == owner_index[None, :]) & (
        position[:, None] >= position[None, :]
    )
    bias_flat = qkv_bias.astype(jnp.float32).reshape(-1)
    gathered = lax.all_gather(hidden_in, "narrow", axis=1, tiled=True)
    carried = hidden_in
    appended = []
    for layer_index in range(LAYERS):
        projections = add_rows(lax.all_gather(w_qkv, "wide", axis=0, tiled=True), operand=gathered)
        projections = projections + bias_flat
        queries = projections[:, :local_width].astype(jnp.bfloat16)
        keys_new = projections[:, local_width : 2 * local_width].astype(jnp.bfloat16)
        values_new = projections[:, 2 * local_width :].astype(jnp.bfloat16)
        appended.append(jnp.stack([keys_new, values_new]))
        keys_cache = cache_kv[layer_index, 0].reshape(cache_count, local_heads, HEAD)
        values_cache = cache_kv[layer_index, 1].reshape(cache_count, local_heads, HEAD)
        attended = attend(
            queries.reshape(row_count, local_heads, HEAD),
            keys_new.reshape(row_count, local_heads, HEAD),
            values_new.reshape(row_count, local_heads, HEAD),
            keys_cache,
            values_cache,
            live_cache,
            live_new,
        )
        heads_all = lax.all_gather(attended, "narrow", axis=1, tiled=True)
        projected = add_rows(lax.all_gather(w_out, "wide", axis=0, tiled=True), operand=heads_all)
        summed = (projected + out_bias.astype(jnp.float32) + carried.astype(jnp.float32)).astype(
            jnp.bfloat16
        )
        if layer_index + 1 < LAYERS:
            carried = norm_slice(summed, norm_gain, norm_shift, full_width)
            gathered = lax.all_gather(carried, "narrow", axis=1, tiled=True)
        else:
            carried = norm_slice(summed, norm_gain, norm_shift, full_width)
    return (carried, jnp.stack(appended))


def solution(mesh):
    in_specs = (
        P("wide", "narrow"),
        P("wide"),
        P("wide"),
        P(None, None, "wide", "narrow"),
        P("wide", None, "narrow"),
        P(None, "narrow"),
        P("wide", "narrow"),
        P("narrow"),
        P("narrow"),
        P("narrow"),
    )
    out_specs = (P("wide", "narrow"), P(None, None, "wide", "narrow"))
    return jax.shard_map(shards, mesh=mesh, in_specs=in_specs, out_specs=out_specs, check_vma=False)
```

profile of v0, /device:TPU:0, one launch (start us, length us, event | category | flops | bytes accessed | tf_op | source)
XLA Modules:
  0.0 317.0 jit_solution(13035055456432383574)
XLA Ops:
  7.2 0.7 all-gather.7.cloned.1.call-update
  7.9 2.3 copy.24
  10.3 0.7 all-gather.13.cloned.1.call-update
  11.0 5.7 %fusion.66 = (bf16[1,1,1024,1024]{3,2,1,0:T(8,128)(2,1)}, bf16[1,1,1024,1024]{3,2,1,0:T(8,128)(2,1)}, bf16[1,1,1024,1024]{3,2,1,0:T(8,128)(2,1)}, bf16[1,1,1024,1024]{3,2,1,0:T(8,128)(2,1)S(1)}) fusion(bf16[2,2,1024,1024]{3,2,1,0:T(8,128)(2,1)} %param.13), kind=kLoop, calls=%fused_computation.113 | loop fusion | bytes 16777216 | tf_op jit(solution)/shard_map/slice | solution.py:104
  16.7 2.6 copy.30
  19.3 2.9 copy.47
  22.4 0.1 compare_and_fusion.1
  22.6 0.3 compare_and_fusion
  22.9 10.7 %all-gather.7.cloned.1.call-done = bf16[256,2048]{1,0:T(8,128)(2,1)} async-done(((bf16[256,1024]{1,0:T(8,128)(2,1)}), bf16[256,2048]{1,0:T(8,128)(2,1)}) %all-gather.7.cloned.1.call-update) | async-done | bytes 1048592 | tf_op jit(solution)/shard_map/all_gather | solution.py:94
  33.6 106.1 %all-gather.9.cloned.1.call-done = bf16[2048,3,1024]{0,2,1:T(8,128)(2,1)} async-done(((bf16[128,3,1024]{0,2,1:T(8,128)(2,1)}), bf16[2048,3,1024]{0,2,1:T(8,128)(2,1)}) %all-gather.9.cloned.1.call-update) | async-done | bytes 12582928 | tf_op jit(solution)/shard_map/all_gather | solution.py:98
  139.7 8.4 %fusion.6 = bf16[256,3072]{1,0:T(8,128)(2,1)S(1)} fusion(bf16[256,2048]{1,0:T(8,128)(2,1)} %all-gather.7.cloned.1.call-done, bf16[2048,3072]{0,1:T(8,128)(2,1)} %bitcast.100, f32[3072]{0:T(1024)S(1)} %reshape.251), kind=kOutput, calls=%fused_computation.14 | convolution fusion | flops 3222798336 | bytes 15216640 | tf_op jit(solution)/shard_map/dot_general | solution.py:19
  148.1 1.4 slice_bitcast_fusion.4
  149.5 1.0 copy.45
  150.5 1.5 fusion.8
  152.0 1.9 fusion
  153.9 0.5 fusion.10
  154.4 2.7 fusion.2
  157.2 2.7 fusion.13
  159.9 1.6 fusion.20
  161.7 29.0 %all-gather.13.cloned.1.call-done = bf16[2048,1024]{1,0:T(8,128)(2,1)} async-done(((bf16[128,1024]{1,0:T(8,128)(2,1)}), bf16[2048,1024]{1,0:T(8,128)(2,1)}) %all-gather.13.cloned.1.call-update) | async-done | bytes 4194320 | tf_op jit(solution)/shard_map/all_gather | solution.py:116
  190.7 21.8 %all-gather.11.cloned.1.call-done = bf16[256,2048]{0,1:T(8,128)(2,1)} async-done(((bf16[256,1024]{0,1:T(8,128)(2,1)}), bf16[256,2048]{0,1:T(8,128)(2,1)}) %all-gather.11.cloned.1.call-update) | async-done | bytes 1048592 | tf_op jit(solution)/shard_map/all_gather | solution.py:115
  212.5 3.9 %convert_reduce_fusion.1 = (f32[256]{0:T(256)S(1)}, bf16[256,1024]{1,0:T(8,128)(2,1)S(1)}) fusion(bf16[256,1024]{1,0:T(8,128)(2,1)S(1)} %copy-done.10, f32[1024]{0:T(1024)S(1)} %convert_element_type.64, bf16[256,2048]{0,1:T(8,128)(2,1)} %all-gather.11.cloned.1.call-done, bf16[2048,1024]{1,0:T(8,128)(2,1)} %all-gather.13.cloned.1.call-done), kind=kOutput, calls=%fused_computation.36 | convolution fusion | flops 1075314432 | bytes 6296576 | tf_op jit(solution)/shard_map/dot_general | solution.py:19
  216.4 5.1 %psum.28 = f32[256]{0:T(256)S(1)} all-reduce(f32[256]{0:T(256)S(1)} %get-tuple-element.20), channel_id=1, replica_groups=mesh['wide'=16,'narrow'=2] {'narrow'}, use_global_device_ids=true, to_apply=%region_5.6 | all-reduce | flops 256 | bytes 2048 | tf_op jit(solution)/shard_map/psum | solution.py:24
  221.4 0.3 fusion.30
  221.7 4.9 %psum.29 = f32[256]{0:T(256)S(1)} all-reduce(f32[256]{0:T(256)S(1)} %fusion.30), channel_id=1, replica_groups=mesh['wide'=16,'narrow'=2] {'narrow'}, use_global_device_ids=true, to_apply=%region_7.8 | all-reduce | flops 256 | bytes 2048 | tf_op jit(solution)/shard_map/psum | solution.py:26
  226.7 1.1 fusion.33
  227.8 2.6 copy.38
  230.4 2.9 copy.48
  233.3 16.0 %all-gather.15.cloned.1.call-done = bf16[256,2048]{1,0:T(8,128)(2,1)} async-done(((bf16[256,1024]{1,0:T(8,128)(2,1)}), bf16[256,2048]{1,0:T(8,128)(2,1)}) %all-gather.15.cloned.1.call-update) | async-done | bytes 1048592 | tf_op jit(solution)/shard_map/all_gather | solution.py:122
  249.3 8.4 %fusion.7 = bf16[256,3072]{1,0:T(8,128)(2,1)S(1)} fusion(bf16[256,2048]{1,0:T(8,128)(2,1)} %all-gather.15.cloned.1.call-done, bf16[2048,3072]{0,1:T(8,128)(2,1)} %bitcast.101, f32[3072]{0:T(1024)S(1)} %reshape.251), kind=kOutput, calls=%fused_computation.15 | convolution fusion | flops 3222798336 | bytes 15216640 | tf_op jit(solution)/shard_map/dot_general | solution.py:19
  257.6 1.2 slice_bitcast_fusion.2
  258.8 1.9 fusion.1
  260.7 0.5 fusion.9
  261.2 2.7 fusion.3
  263.9 0.8 copy-done.4
  264.7 0.5 fusion.11
  265.2 1.0 copy.46
  266.2 5.6 %fusion.12 = f32[256,8,128]{0,2,1:T(8,128)S(1)} fusion(bf16[1024,8,128]{0,2,1:T(8,128)(2,1)S(1)} %bitcast.95, f32[8,256,1024]{2,1,0:T(8,128)} %copy-done, f32[8,256]{1,0:T(8,128)S(1)} %add.154, f32[8,256]{1,0:T(8,128)S(1)} %max.15, pred[256,1024]{1,0:T(8,128)(4,1)S(1)} %compare_and_fusion), kind=kOutput, calls=%fused_computation.27 | convolution fusion | flops 549453824 | bytes 11812864 | tf_op jit(solution)/shard_map/hqk,khd->qhd/dot_general | solution.py:53
  271.9 1.6 fusion.21
  273.6 0.1 maximum_bitcast_fusion
  273.7 0.9 copy-done.9
  274.7 1.5 pad_maximum_fusion
  276.2 18.8 %all-gather.17.cloned.1.call-done = bf16[256,2048]{0,1:T(8,128)(2,1)} async-done(((bf16[256,1024]{0,1:T(8,128)(2,1)}), bf16[256,2048]{0,1:T(8,128)(2,1)}) %all-gather.17.cloned.1.call-update) | async-done | bytes 1048592 | tf_op jit(solution)/shard_map/all_gather | solution.py:115
  295.0 3.9 %convert_reduce_fusion = (f32[256]{0:T(256)S(1)}, bf16[256,1024]{1,0:T(8,128)(2,1)S(1)}) fusion(bf16[256,1024]{1,0:T(8,128)(2,1)S(1)} %copy-done.6, f32[1024]{0:T(1024)S(1)} %convert_element_type.64, bf16[256,2048]{0,1:T(8,128)(2,1)} %all-gather.17.cloned.1.call-done, bf16[2048,1024]{1,0:T(8,128)(2,1)} %all-gather.13.cloned.1.call-done), kind=kOutput, calls=%fused_computation.34 | convolution fusion | flops 1075314432 | bytes 6296576 | tf_op jit(solution)/shard_map/dot_general | solution.py:19
  298.9 4.9 %psum.30 = f32[256]{0:T(256)S(1)} all-reduce(f32[256]{0:T(256)S(1)} %get-tuple-element.26), channel_id=1, replica_groups=mesh['wide'=16,'narrow'=2] {'narrow'}, use_global_device_ids=true, to_apply=%region_13.14 | all-reduce | flops 256 | bytes 2048 | tf_op jit(solution)/shard_map/psum | solution.py:24
  303.9 0.3 fusion.26
  304.2 4.9 %psum.31 = f32[256]{0:T(256)S(1)} all-reduce(f32[256]{0:T(256)S(1)} %fusion.26), channel_id=1, replica_groups=mesh['wide'=16,'narrow'=2] {'narrow'}, use_global_device_ids=true, to_apply=%region_15.16 | all-reduce | flops 256 | bytes 2048 | tf_op jit(solution)/shard_map/psum | solution.py:26
  309.1 1.1 fusion.29
  (63 shorter events, 0.7 us)
Async XLA Ops:
  7.2 26.4 %all-gather.7.cloned.1.call-start = ((), (), s32[]{:S(2)}) async-start(), calls=%async_computation | async-start | bytes 1572864 | tf_op jit(solution)/shard_map/all_gather | solution.py:94
  7.9 131.8 %all-gather.9.cloned.1.call-start = ((), (), s32[]{:S(2)}) async-start(), calls=%async_computation.1 | async-start | bytes 13369344 | tf_op jit(solution)/shard_map/all_gather | solution.py:98
  10.2 180.4 %all-gather.13.cloned.1.call-start = ((), (), s32[]{:S(2)}) async-start(), calls=%async_computation.3 | async-start | bytes 4456448 | tf_op jit(solution)/shard_map/all_gather | solution.py:116
  11.0 201.5 %all-gather.11.cloned.1.call-start = ((), (), s32[]{:S(2)}) async-start(), calls=%async_computation.2 | async-start | bytes 1572864 | tf_op jit(solution)/shard_map/all_gather | solution.py:115
  19.3 2.9 copy-start.13
  19.3 3.0 copy-start.18
  19.3 3.1 copy-start.17
  154.4 2.8 copy-start.2
  157.2 2.7 copy-start.11
  159.9 1.7 copy-start.14
  159.9 1.7 copy-start.15
  159.9 1.8 copy-start.16
  159.9 52.5 %copy-start.10 = (bf16[256,1024]{1,0:T(8,128)(2,1)S(1)}, bf16[256,1024]{1,0:T(8,128)(2,1)}, u32[]{:S(2)}) copy-start(bf16[256,1024]{1,0:T(8,128)(2,1)} %param.10) | copy-start | bytes 1572868
  161.6 87.7 %all-gather.15.cloned.1.call-start = ((), (), s32[]{:S(2)}) async-start(), calls=%async_computation.4 | async-start | bytes 1572864 | tf_op jit(solution)/shard_map/all_gather | solution.py:122
  216.4 11.5 %copy-start.1 = (bf16[1,1,1024,1024]{3,2,1,0:T(8,128)(2,1)S(1)}, bf16[1,1,1024,1024]{3,2,1,0:T(8,128)(2,1)}, u32[]{:S(2)}) copy-start(bf16[1,1,1024,1024]{3,2,1,0:T(8,128)(2,1)} %get-tuple-element.4) | copy-start | bytes 6291460
  227.8 67.3 %all-gather.17.cloned.1.call-start = ((), (), s32[]{:S(2)}) async-start(), calls=%async_computation.5 | async-start | bytes 1572864 | tf_op jit(solution)/shard_map/all_gather | solution.py:115
  260.7 3.2 %copy-start = (f32[8,256,1024]{2,1,0:T(8,128)}, f32[8,256,1024]{2,1,0:T(8,128)S(1)}, u32[]{:S(2)}) copy-start(f32[8,256,1024]{2,1,0:T(8,128)S(1)} %get-tuple-element.23) | copy-start | bytes 25165828
  261.2 3.5 %copy-start.4 = (f32[8,256,256]{1,2,0:T(8,128)}, f32[8,256,256]{1,2,0:T(8,128)S(1)}, u32[]{:S(2)}) copy-start(f32[8,256,256]{1,2,0:T(8,128)S(1)} %get-tuple-element.25) | copy-start | bytes 6291460
  263.9 2.3 copy-start.3
  266.2 5.7 %copy-start.5 = (f32[8,256,256]{1,2,0:T(8,128)S(1)}, f32[8,256,256]{1,2,0:T(8,128)}, u32[]{:S(2)}) copy-start(f32[8,256,256]{1,2,0:T(8,128)} %copy-done.4) | copy-start | bytes 6291460
  266.2 5.7 %copy-start.12 = (bf16[256,1024]{0,1:T(8,128)(2,1)S(1)}, bf16[256,1024]{0,1:T(8,128)(2,1)}, u32[]{:S(2)}) copy-start(bf16[256,1024]{0,1:T(8,128)(2,1)} %copy.46) | copy-start | bytes 1572868
  271.9 1.7 copy-start.7
  271.9 1.7 copy-start.8
  273.6 1.0 copy-start.9
  274.7 20.4 %copy-start.6 = (bf16[256,1024]{1,0:T(8,128)(2,1)S(1)}, bf16[256,1024]{1,0:T(8,128)(2,1)}, u32[]{:S(2)}) copy-start(bf16[256,1024]{1,0:T(8,128)(2,1)} %fusion.33) | copy-start | bytes 1572868
Sparse Core Ops, SparseCore 0:
  9.5 23.9 all-gather.6
  35.7 103.9 all-gather.8
  141.9 48.7 all-gather.12
  192.6 19.7 all-gather.10
  227.9 21.3 all-gather.14
  273.7 21.2 all-gather.16
where the time goes:
time: 318 us; the launch traced here: 317 us
  waiting for transfers between devices  204 us (64%)
  matrix products  41.8 us (13%)
  local copies, waits for them, and re-layouts  25.3 us (8%)
  blocking collectives  19.9 us (6%)
  between operations  14.5 us (5%)
  other arithmetic  11.4 us (4%)
    all_gather x1, waiting for transfers between devices, shards(): lax.all_gather(w_qkv, 'wide', axis=0, tiled=True)  106 us
    all_gather x2, waiting for transfers between devices, shards(): heads_all = lax.all_gather(attended, 'narrow', axis=1, tiled=True)  40.6 us
    all_gather x1, waiting for transfers between devices, shards(): lax.all_gather(w_out, 'wide', axis=0, tiled=True)  29 us
    dot_general x4, matrix products, add_rows(): jnp.dot(operand, shard_piece.reshape(piece_rows, -1), preferred_element_t...  24.5 us
    all_gather x1, waiting for transfers between devices, shards(): gathered = lax.all_gather(carried, 'narrow', axis=1, tiled=True)  16 us
    all_gather x1, waiting for transfers between devices, shards(): gathered = lax.all_gather(hidden_in, 'narrow', axis=1, tiled=True)  10.7 us
    psum x2, blocking collectives, norm_slice(): row_means = lax.psum(jnp.sum(values, axis=1), 'narrow') / full_width  10 us
    psum x2, blocking collectives, norm_slice(): lax.psum(jnp.sum(centered * centered, axis=1), 'narrow') / full_width  9.88 us
  transfers between devices with their start and end apart: 6, of which 6 were waited for; matrix products, arithmetic and copies ran while one was open for 14% of the time, Pallas kernels for 0%

commit v1 on v0

--- a/solution.py
+++ b/solution.py
@@ -1,8 +1,11 @@
+import functools
 import math
 
 import jax
 import jax.numpy as jnp
 from jax import lax
+from jax.experimental import pallas as pl
+from jax.experimental.pallas import tpu as pltpu
 from jax.sharding import PartitionSpec as P
 
 HEAD = 128
@@ -125,6 +128,484 @@
     return (carried, jnp.stack(appended))
 
 
+MESH = pl.DeviceIdType.MESH
+CHIPS_Y = 2
+CHIPS_Z = 4
+CORES = 2
+UP, DOWN, ACROSS, SIBLING = range(4)
+QKV, OUT = range(2)
+FIRST, SECOND = range(2)
+VMEM_BYTES = 58 * 1024 * 1024
+
+
+def fits_fused(mesh):
+    return mesh.shape["wide"] == CHIPS_Z * CHIPS_Y * CORES and mesh.shape["narrow"] == 2
+
+
+class Gather:
+    def __init__(self, buffers, shard_rows, cuts, send_sem, recv_sem):
+        self.buffers, self.shard_rows, self.cuts = buffers, shard_rows, cuts
+        self.send_sem, self.recv_sem = send_sem, recv_sem
+        me = lax.axis_index("wide")
+        self.core = lax.rem(me, CORES)
+        self.y = lax.rem(me // CORES, CHIPS_Y)
+        self.z = me // (CORES * CHIPS_Y)
+        self.me = me
+        self.targets = {
+            UP: (self.z + 1 < CHIPS_Z, me + CORES * CHIPS_Y),
+            DOWN: (self.z > 0, me - CORES * CHIPS_Y),
+            ACROSS: (True, self.index(self.z, 1 - self.y, self.core)),
+            SIBLING: (True, self.index(self.z, self.y, 1 - self.core)),
+        }
+        self.pending = []
+
+    def index(self, z, y, core):
+        return (z * CHIPS_Y + y) * CORES + core
+
+    def slot(self, which, part, source):
+        cut = self.cuts[which]
+        start = source * self.shard_rows + (0 if part == FIRST else cut)
+        size = cut if part == FIRST else self.shard_rows - cut
+        return self.buffers[which].at[pl.ds(pl.multiple_of(start, 16), size), :]
+
+    def copy(self, which, part, z, y, core, kind):
+        source = self.index(z, y, core)
+        block = self.slot(which, part, source)
+        return pltpu.make_async_remote_copy(
+            src_ref=block,
+            dst_ref=block,
+            send_sem=self.send_sem.at[which, part, z * CHIPS_Y + y, kind],
+            recv_sem=self.recv_sem.at[which, part, source],
+            device_id={"wide": self.targets[kind][1]},
+            device_id_type=MESH,
+        )
+
+    def send(self, which, part, z, y, kinds, valid=True):
+        for kind in kinds:
+            condition = self.targets[kind][0]
+            if condition is True:
+                condition = valid
+            elif valid is not True:
+                condition = jnp.logical_and(condition, valid)
+            make = functools.partial(self.copy, which, part, z, y, self.core, kind)
+            self.when(condition, lambda make=make: make().start())
+            self.pending.append((condition, make))
+
+    def when(self, condition, action):
+        if condition is True:
+            action()
+        else:
+            pl.when(condition)(action)
+
+    def arrive(self, which, part, z, y, core, valid=True):
+        make = functools.partial(self.copy, which, part, z, y, core, SIBLING)
+        self.when(valid, lambda: make().wait_recv())
+
+    def begin(self, which):
+        z, y = self.z, self.y
+        self.send(which, SECOND, z, y, (ACROSS,))
+        self.send(which, FIRST, z, y, (UP, DOWN, ACROSS))
+        self.send(which, SECOND, z, y, (UP, DOWN))
+        self.send(which, FIRST, z, y, (SIBLING,))
+        self.send(which, SECOND, z, y, (SIBLING,))
+
+    def around(self, distance):
+        low, high = self.z - distance, self.z + distance
+        return ((low, low >= 0, UP), (high, high < CHIPS_Z, DOWN))
+
+    def take_across(self, which, distance):
+        y = 1 - self.y
+        places = ((self.z, True, None),) if distance == 0 else self.around(distance)
+        for z, valid, _ in places:
+            self.arrive(which, FIRST, z, y, self.core, valid)
+            self.send(which, FIRST, z, y, (SIBLING,), valid)
+
+    def step(self, which, distance):
+        if distance == 0:
+            y = 1 - self.y
+            self.arrive(which, SECOND, self.z, y, self.core)
+            self.send(which, SECOND, self.z, y, (UP, DOWN, SIBLING))
+            return
+        if distance < CHIPS_Z:
+            for z, valid, onward in self.around(distance):
+                self.arrive(which, FIRST, z, self.y, self.core, valid)
+                self.send(which, FIRST, z, self.y, (onward, ACROSS, SIBLING), valid)
+            for z, valid, onward in self.around(distance):
+                for y in (self.y, 1 - self.y):
+                    self.arrive(which, SECOND, z, y, self.core, valid)
+                    self.send(which, SECOND, z, y, (onward, SIBLING), valid)
+        self.take_across(which, distance - 1)
+
+    def finish(self, which):
+        for part in (FIRST, SECOND):
+            for z in range(CHIPS_Z):
+                for y in range(CHIPS_Y):
+                    self.arrive(which, part, z, y, 1 - self.core)
+
+    def drain(self):
+        for condition, make in self.pending:
+            self.when(condition, lambda make=make: make().wait_send())
+
+
+def fused_kernel(
+    lengths,
+    offsets,
+    hidden,
+    cache,
+    w_qkv,
+    w_out,
+    qkv_bias,
+    out_bias,
+    scales,
+    hidden_out,
+    new_cache,
+    qkv_rows,
+    out_rows,
+    cache_here,
+    inputs,
+    projected,
+    attended,
+    summed,
+    normed,
+    scales_all,
+    stats,
+    live,
+    send_sem,
+    recv_sem,
+    local_sem,
+    side_send,
+    side_recv,
+):
+    tokens, width = hidden.shape
+    cache_count = cache.shape[2]
+    requests = lengths.shape[0]
+    shard_rows = w_qkv.shape[0]
+    heads = width // HEAD
+    full_width = 2 * width
+    column = lax.axis_index("narrow")
+    other = 1 - column
+    gather = Gather((qkv_rows, out_rows), shard_rows, (112, 96), send_sem, recv_sem)
+
+    barrier = pltpu.get_barrier_semaphore()
+    for condition, target in gather.targets.values():
+
+        def greet(target=target):
+            pl.semaphore_signal(
+                barrier, inc=1, device_id={"wide": target}, device_id_type=MESH
+            )
+
+        gather.when(condition, greet)
+    pl.semaphore_signal(barrier, inc=1, device_id={"narrow": other}, device_id_type=MESH)
+
+    own_rows = pl.ds(pl.multiple_of(gather.me * shard_rows, 16), shard_rows)
+    load_qkv = pltpu.make_async_copy(w_qkv, qkv_rows.at[own_rows, :], local_sem.at[0])
+    load_out = pltpu.make_async_copy(w_out, out_rows.at[own_rows, :], local_sem.at[1])
+    load_hidden = pltpu.make_async_copy(hidden, inputs.at[column], local_sem.at[2])
+    load_cache = pltpu.make_async_copy(cache, cache_here, local_sem.at[3])
+    load_scales = pltpu.make_async_copy(scales, scales_all.at[column], local_sem.at[4])
+    for load in (load_qkv, load_out, load_hidden, load_scales, load_cache):
+        load.start()
+
+    has_lower = (gather.z + CHIPS_Z - 1) // CHIPS_Z
+    has_upper = (2 * CHIPS_Z - 2 - gather.z) // CHIPS_Z
+    pl.semaphore_wait(barrier, 3 + has_lower + has_upper)
+
+    def beside(source, target, number):
+        return pltpu.make_async_remote_copy(
+            src_ref=source,
+            dst_ref=target,
+            send_sem=side_send.at[number],
+            recv_sem=side_recv.at[number],
+            device_id={"narrow": other},
+            device_id_type=MESH,
+        )
+
+    load_qkv.wait()
+    gather.begin(QKV)
+    load_hidden.wait()
+    load_scales.wait()
+    send_hidden = beside(inputs.at[column], inputs.at[column], 0)
+    send_scales = beside(scales_all.at[column], scales_all.at[column], 1)
+    send_hidden.start()
+    send_scales.start()
+    load_out.wait()
+    sides = [send_hidden, send_scales]
+
+    block_start = gather.me * cache_count
+    rows_global = block_start + lax.broadcasted_iota(jnp.int32, (8, cache_count), 1)
+    for request in range(requests):
+        start = offsets[request]
+        stop = start + lengths[request]
+        alive = jnp.logical_and(rows_global >= start, rows_global < stop)
+        live[request] = jnp.where(alive, 0.0, NEGATIVE)
+    later = lax.broadcasted_iota(jnp.int32, (SPAN, SPAN), 0) < lax.broadcasted_iota(
+        jnp.int32, (SPAN, SPAN), 1
+    )
+    scale_factor = 1.0 / math.sqrt(HEAD)
+
+    for distance in range(CHIPS_Z):
+        gather.step(QKV, distance)
+    gather.begin(OUT)
+    gather.step(QKV, CHIPS_Z)
+    gather.finish(QKV)
+    send_hidden.wait_recv()
+    send_scales.wait_recv()
+    load_cache.wait()
+
+    tile = 512
+
+    def project(layer, source):
+        def one(j, carry):
+            columns = pl.ds(pl.multiple_of(j * tile, tile), tile)
+            total = jnp.dot(
+                source[0], qkv_rows[:width, columns], preferred_element_type=jnp.float32
+            )
+            total += jnp.dot(
+                source[1], qkv_rows[width:, columns], preferred_element_type=jnp.float32
+            )
+            projected[layer, :, columns] = (total + qkv_bias[:, columns]).astype(jnp.bfloat16)
+            return carry
+
+        lax.fori_loop(0, 3 * width // tile, one, 0)
+        stores = []
+        for kind in range(2):
+            block = projected.at[layer, :, (kind + 1) * width : (kind + 2) * width]
+            store = pltpu.make_async_copy(
+                block, new_cache.at[layer, kind], local_sem.at[5 + 2 * layer + kind]
+            )
+            store.start()
+            stores.append(store)
+        return stores
+
+    def attend_heads(layer, first, count):
+        def one(head, carry):
+            place = head * HEAD
+            here = pl.ds(pl.multiple_of(place, HEAD), HEAD)
+            key_columns = pl.ds(pl.multiple_of(place + width, HEAD), HEAD)
+            value_columns = pl.ds(pl.multiple_of(place + 2 * width, HEAD), HEAD)
+            keys_cached = cache_here[layer, 0, :, here]
+            values_cached = cache_here[layer, 1, :, here]
+            for request in range(requests):
+                rows = slice(request * SPAN, (request + 1) * SPAN)
+                queries = projected[layer, rows, here]
+                keys_new = projected[layer, rows, key_columns]
+                values_new = projected[layer, rows, value_columns]
+                contract = (((1,), (1,)), ((), ()))
+                scores_cache = lax.dot_general(
+                    queries, keys_cached, contract, preferred_element_type=jnp.float32
+                )
+                scores_new = lax.dot_general(
+                    queries, keys_new, contract, preferred_element_type=jnp.float32
+                )
+                scores_cache = scores_cache * scale_factor + live[request, 0:1, :]
+                scores_new = jnp.where(later, NEGATIVE, scores_new * scale_factor)
+                top = jnp.maximum(
+                    jnp.max(scores_cache, axis=1, keepdims=True),
+                    jnp.max(scores_new, axis=1, keepdims=True),
+                )
+                weights_cache = jnp.exp(scores_cache - top)
+                weights_new = jnp.exp(scores_new - top)
+                totals = jnp.sum(weights_cache, axis=1, keepdims=True) + jnp.sum(
+                    weights_new, axis=1, keepdims=True
+                )
+                combined = jnp.dot(
+                    weights_cache.astype(jnp.bfloat16),
+                    values_cached,
+                    preferred_element_type=jnp.float32,
+                )
+                combined += jnp.dot(
+                    weights_new.astype(jnp.bfloat16),
+                    values_new,
+                    preferred_element_type=jnp.float32,
+                )
+                attended[layer, column, rows, here] = (combined / totals).astype(jnp.bfloat16)
+            return carry
+
+        lax.fori_loop(first, first + count, one, 0)
+
+    group = 2
+
+    def attend_all(layer, between):
+        copies = []
+        for number, first in enumerate(range(0, heads, group)):
+            attend_heads(layer, first, group)
+            block = attended.at[layer, column, :, first * HEAD : (first + group) * HEAD]
+            copy = beside(block, block, 2 + layer * 4 + number)
+            copy.start()
+            copies.append(copy)
+            between(number)
+        return copies
+
+    def mix(layer, carried, after):
+        for number in range(width // tile):
+            columns = slice(number * tile, (number + 1) * tile)
+            total = jnp.dot(
+                attended[layer, 0], out_rows[:width, columns], preferred_element_type=jnp.float32
+            )
+            total += jnp.dot(
+                attended[layer, 1], out_rows[width:, columns], preferred_element_type=jnp.float32
+            )
+            total = total + out_bias[:, columns] + carried[column, :, columns].astype(jnp.float32)
+            summed[layer, column, :, columns] = total.astype(jnp.bfloat16)
+            after(number, columns)
+
+    stores = project(0, inputs)
+    gather.step(OUT, 0)
+
+    def advance(number):
+        gather.step(OUT, number + 1)
+
+    copies = attend_all(0, advance)
+    gather.finish(OUT)
+    for copy in copies:
+        copy.wait_recv()
+    sides += copies
+
+    exchanged = []
+
+    def share(number, columns):
+        block = summed.at[0, column, :, columns]
+        copy = beside(block, block, 10 + number)
+        copy.start()
+        exchanged.append(copy)
+
+    mix(0, inputs, share)
+    for copy in exchanged:
+        copy.wait_recv()
+    sides += exchanged
+
+    chunk = 64
+
+    def norm_rows(j, carry):
+        rows = pl.ds(pl.multiple_of(j * chunk, chunk), chunk)
+        values = [summed[0, half, rows, :].astype(jnp.float32) for half in range(2)]
+        means = sum(jnp.sum(v, axis=1, keepdims=True) for v in values) / full_width
+        centered = [v - means for v in values]
+        spread = sum(jnp.sum(c * c, axis=1, keepdims=True) for c in centered) / full_width
+        inverse = lax.rsqrt(spread + EPSILON)
+        for half in range(2):
+            scaled = centered[half] * inverse
+            scaled = scaled * scales_all[half, 0:1, :] + scales_all[half, 1:2, :]
+            normed[half, rows, :] = scaled.astype(jnp.bfloat16)
+        return carry
+
+    lax.fori_loop(0, tokens // chunk, norm_rows, 0)
+
+    stores += project(1, normed)
+    copies = attend_all(1, lambda number: None)
+    for copy in copies:
+        copy.wait_recv()
+    sides += copies
+    mix(1, normed, lambda number, columns: None)
+
+    lane = lax.broadcasted_iota(jnp.int32, (chunk, 128), 1)
+
+    def stat_rows(j, carry):
+        rows = pl.ds(pl.multiple_of(j * chunk, chunk), chunk)
+        values = summed[1, column, rows, :].astype(jnp.float32)
+        mean = jnp.sum(values, axis=1, keepdims=True) / width
+        centered = values - mean
+        spread = jnp.sum(centered * centered, axis=1, keepdims=True)
+        stats[column, rows, :] = jnp.where(lane == 0, mean, jnp.where(lane == 1, spread, 0.0))
+        return carry
+
+    lax.fori_loop(0, tokens // chunk, stat_rows, 0)
+    send_stats = beside(stats.at[column], stats.at[column], 12)
+    send_stats.start()
+    send_stats.wait_recv()
+    sides.append(send_stats)
+
+    def last_rows(j, carry):
+        rows = pl.ds(pl.multiple_of(j * chunk, chunk), chunk)
+        mean_a, mean_b = stats[0, rows, 0:1], stats[1, rows, 0:1]
+        means = (mean_a + mean_b) * 0.5
+        gap = mean_a - mean_b
+        spread = stats[0, rows, 1:2] + stats[1, rows, 1:2] + gap * gap * (width * 0.5)
+        inverse = lax.rsqrt(spread / full_width + EPSILON)
+        scaled = (summed[1, column, rows, :].astype(jnp.float32) - means) * inverse
+        scaled = scaled * scales_all[column, 0:1, :] + scales_all[column, 1:2, :]
+        hidden_out[rows, :] = scaled.astype(jnp.bfloat16)
+        return carry
+
+    lax.fori_loop(0, tokens // chunk, last_rows, 0)
+
+    for store in stores:
+        store.wait()
+    for copy in sides:
+        copy.wait_send()
+    gather.drain()
+
+
+def fused(
+    hidden_in,
+    cache_lengths,
+    cache_offsets,
+    cache_kv,
+    w_qkv,
+    qkv_bias,
+    w_out,
+    out_bias,
+    norm_gain,
+    norm_shift,
+):
+    tokens, width = hidden_in.shape
+    cache_count = cache_kv.shape[2]
+    shard_rows = w_qkv.shape[0]
+    depth = shard_rows * lax.axis_size("wide")
+    requests = cache_lengths.shape[0]
+    scales = jnp.stack([norm_gain, norm_shift]).astype(jnp.float32)
+    scales = jnp.concatenate([scales, jnp.zeros((6, width), jnp.float32)])
+    smem = pl.BlockSpec(memory_space=pltpu.SMEM)
+    vmem = pl.BlockSpec(memory_space=pltpu.VMEM)
+    anywhere = pl.BlockSpec(memory_space=pl.ANY)
+    bf16 = jnp.bfloat16
+    return pl.pallas_call(
+        fused_kernel,
+        out_shape=(
+            jax.ShapeDtypeStruct((tokens, width), bf16),
+            jax.ShapeDtypeStruct((LAYERS, 2, tokens, width), bf16),
+        ),
+        in_specs=[smem, smem, anywhere, anywhere, anywhere, anywhere, vmem, vmem, anywhere],
+        out_specs=(vmem, anywhere),
+        scratch_shapes=[
+            pltpu.VMEM((depth, 3 * width), bf16),
+            pltpu.VMEM((depth, width), bf16),
+            pltpu.VMEM((LAYERS, 2, cache_count, width), bf16),
+            pltpu.VMEM((2, tokens, width), bf16),
+            pltpu.VMEM((LAYERS, tokens, 3 * width), bf16),
+            pltpu.VMEM((LAYERS, 2, tokens, width), bf16),
+            pltpu.VMEM((LAYERS, 2, tokens, width), bf16),
+            pltpu.VMEM((2, tokens, width), bf16),
+            pltpu.VMEM((2, 8, width), jnp.float32),
+            pltpu.VMEM((2, tokens, 128), jnp.float32),
+            pltpu.VMEM((requests, 8, cache_count), jnp.float32),
+            pltpu.SemaphoreType.DMA((2, 2, CHIPS_Z * CHIPS_Y, 4)),
+            pltpu.SemaphoreType.DMA((2, 2, CHIPS_Z * CHIPS_Y * CORES)),
+            pltpu.SemaphoreType.DMA((9,)),
+            pltpu.SemaphoreType.DMA((13,)),
+            pltpu.SemaphoreType.DMA((13,)),
+        ],
+        compiler_params=pltpu.CompilerParams(
+            collective_id=0, has_side_effects=True, vmem_limit_bytes=VMEM_BYTES
+        ),
+        cost_estimate=pl.CostEstimate(
+            flops=2 * LAYERS * tokens * depth * 4 * width,
+            bytes_accessed=2 * depth * 4 * width,
+            transcendentals=LAYERS * tokens * cache_count * (width // HEAD),
+        ),
+    )(
+        cache_lengths,
+        cache_offsets,
+        hidden_in,
+        cache_kv,
+        w_qkv.reshape(shard_rows, 3 * width),
+        w_out,
+        qkv_bias.astype(jnp.float32).reshape(1, 3 * width),
+        out_bias.astype(jnp.float32).reshape(1, width),
+        scales,
+    )
+
+
 def solution(mesh):
     in_specs = (
         P("wide", "narrow"),
@@ -139,4 +620,5 @@
         P("narrow"),
     )
     out_specs = (P("wide", "narrow"), P(None, None, "wide", "narrow"))
-    return jax.shard_map(shards, mesh=mesh, in_specs=in_specs, out_specs=out_specs, check_vma=False)
+    body = fused if fits_fused(mesh) else shards
+    return jax.shard_map(body, mesh=mesh, in_specs=in_specs, out_specs=out_specs, check_vma=False)

time: 318 us -> 161 us (0.51)
  waiting for transfers between devices: 204 us -> 0 us
  Pallas kernels: 0 us -> 148 us
  matrix products: 41.8 us -> 0 us
  blocking collectives: 19.9 us -> 0 us
  local copies, waits for them, and re-layouts: 25.3 us -> 9.6 us
  between operations: 14.5 us -> 0.65 us
  other arithmetic: 11.4 us -> 2.6 us
    all_gather x6 -> x0, waiting for transfers between devices: 202 us -> none  [the longest x1 106 us: shards(): lax.all_gather(w_qkv, 'wide', axis=0, tiled=True)]
    pallas_call x0 -> x1, Pallas kernels: none -> 148 us  [fused(): pl.pallas_call(fused_kernel, out_shape=(jax.ShapeDtypeStruct((tokens, wid...]
    dot_general x12 -> x0, matrix products: 41.8 us -> none  [the longest x4 24.5 us: add_rows(): jnp.dot(operand, shard_piece.reshape(piece_rows, -1), preferred_element_t...]
    psum x4 -> x0, blocking collectives: 19.9 us -> none  [the longest x2 10 us: norm_slice(): row_means = lax.psum(jnp.sum(values, axis=1), 'narrow') / full_width]
    slice x3 -> x0, local copies, waits for them, and re-layouts: 10.8 us -> none  [the longest x1 5.71 us: shards(): cache_kv[layer_index, 0].reshape(cache_count, local_heads, HEAD)]
    reduce_sum x6 -> x0, other arithmetic: 6.97 us -> none  [the longest x2 5.38 us: attend(): jnp.sum(weights_cache, axis=2, keepdims=True)]
    unnamed x41 -> x4, local copies, waits for them, and re-layouts: 9.8 us -> 7.06 us
  transfers between devices with their start and end apart: 6 -> 0, of which waited for: 6 -> 0; matrix products, arithmetic and copies ran while one was open for 14% -> 0% of each run, Pallas kernels for 0% -> 0%
where the time goes in v1:
time: 161 us; the launch traced here: 160 us
  Pallas kernels  148 us (92%)
  local copies, waits for them, and re-layouts  9.6 us (6%)
  other arithmetic  2.6 us (2%)
    pallas_call x1, Pallas kernels, fused(): pl.pallas_call(fused_kernel, out_shape=(jax.ShapeDtypeStruct((tokens, wid...  148 us
    unnamed x4, local copies, waits for them, and re-layouts  7.06 us

profile of v1, /device:TPU:0, one launch (start us, length us, event | category | flops | bytes accessed | tf_op | source)
XLA Modules:
  0.0 160.5 jit_solution(5862353093346291926)
XLA Ops:
  0.6 1.3 reshape.24
  1.9 0.7 stack.9
  2.6 0.7 stack.10
  3.3 0.7 convert_bitcast_fusion
  4.0 0.6 copy.15
  4.6 0.6 fusion.3.scales
  5.2 1.5 copy.13
  6.7 1.2 copy.14.w_qkv
  7.9 147.6 %shard_map.113 = (bf16[256,1024]{1,0:T(8,128)(2,1)}, bf16[2,2,256,1024]{3,2,1,0:T(8,128)(2,1)}) custom-call(s32[2]{0:T(128)} %lengths.1, s32[2]{0:T(128)} %offsets.1, bf16[256,1024]{1,0:T(8,128)(2,1)} %hidden.1, bf16[2,2,1024,1024]{3,2,1,0:T(8,128)(2,1)} %cache.1, bf16[128,3072]{1,0:T(8,128)(2,1)} %copy.14.w_qkv, bf16[128,1024]{1,0:T(8,128)(2,1)} %w_out.1, ...), custom_call_target="tpu_custom_call" | custom-call | flops 8589934592 | bytes 16777216 | tf_op jit(solution)/shard_map/pallas_call | solution.py:562
  155.5 1.9 %copy.18 = bf16[256,1024]{1,0:T(8,128)(2,1)} copy(bf16[256,1024]{1,0:T(8,128)(2,1)} %get-tuple-element.4) | data formatting | bytes 1048576
  157.4 3.1 %copy.19 = bf16[2,2,256,1024]{3,2,1,0:T(8,128)(2,1)} copy(bf16[2,2,256,1024]{3,2,1,0:T(8,128)(2,1)} %get-tuple-element.5) | data formatting | bytes 4194304

commit v2 on v1

--- a/solution.py
+++ b/solution.py
@@ -133,9 +133,10 @@
 CHIPS_Z = 4
 CORES = 2
 UP, DOWN, ACROSS, SIBLING = range(4)
-QKV, OUT = range(2)
+QUERY, KEY, VALUE, OUT = range(4)
+QKV = (QUERY, KEY, VALUE)
 FIRST, SECOND = range(2)
-VMEM_BYTES = 58 * 1024 * 1024
+VMEM_BYTES = 48 * 1024 * 1024
 
 
 def fits_fused(mesh):
@@ -166,7 +167,8 @@
         cut = self.cuts[which]
         start = source * self.shard_rows + (0 if part == FIRST else cut)
         size = cut if part == FIRST else self.shard_rows - cut
-        return self.buffers[which].at[pl.ds(pl.multiple_of(start, 16), size), :]
+        buffer, columns = self.buffers[which]
+        return buffer.at[pl.ds(pl.multiple_of(start, 16), size), columns]
 
     def copy(self, which, part, z, y, core, kind):
         source = self.index(z, y, core)
@@ -245,6 +247,7 @@
     def drain(self):
         for condition, make in self.pending:
             self.when(condition, lambda make=make: make().wait_send())
+        self.pending = []
 
 
 def fused_kernel(
@@ -256,7 +259,8 @@
     w_out,
     qkv_bias,
     out_bias,
-    scales,
+    norm_gain,
+    norm_shift,
     hidden_out,
     new_cache,
     qkv_rows,
@@ -268,7 +272,9 @@
     summed,
     normed,
     scales_all,
+    biases,
     stats,
+    stats_wide,
     live,
     send_sem,
     recv_sem,
@@ -279,12 +285,14 @@
     tokens, width = hidden.shape
     cache_count = cache.shape[2]
     requests = lengths.shape[0]
-    shard_rows = w_qkv.shape[0]
+    shard_rows = w_out.shape[0]
     heads = width // HEAD
     full_width = 2 * width
     column = lax.axis_index("narrow")
     other = 1 - column
-    gather = Gather((qkv_rows, out_rows), shard_rows, (112, 96), send_sem, recv_sem)
+    buffers = [(qkv_rows, slice(kind * width, (kind + 1) * width)) for kind in QKV]
+    buffers.append((out_rows, slice(0, width)))
+    gather = Gather(buffers, shard_rows, (112, 112, 112, 96), send_sem, recv_sem)
 
     barrier = pltpu.get_barrier_semaphore()
     for condition, target in gather.targets.values():
@@ -298,12 +306,16 @@
     pl.semaphore_signal(barrier, inc=1, device_id={"narrow": other}, device_id_type=MESH)
 
     own_rows = pl.ds(pl.multiple_of(gather.me * shard_rows, 16), shard_rows)
-    load_qkv = pltpu.make_async_copy(w_qkv, qkv_rows.at[own_rows, :], local_sem.at[0])
+    load_qkv = [
+        pltpu.make_async_copy(
+            w_qkv.at[kind], qkv_rows.at[own_rows, buffers[kind][1]], local_sem.at[9 + kind]
+        )
+        for kind in QKV
+    ]
     load_out = pltpu.make_async_copy(w_out, out_rows.at[own_rows, :], local_sem.at[1])
     load_hidden = pltpu.make_async_copy(hidden, inputs.at[column], local_sem.at[2])
     load_cache = pltpu.make_async_copy(cache, cache_here, local_sem.at[3])
-    load_scales = pltpu.make_async_copy(scales, scales_all.at[column], local_sem.at[4])
-    for load in (load_qkv, load_out, load_hidden, load_scales, load_cache):
+    for load in (*load_qkv, load_hidden, load_out, load_cache):
         load.start()
 
     has_lower = (gather.z + CHIPS_Z - 1) // CHIPS_Z
@@ -320,10 +332,16 @@
             device_id_type=MESH,
         )
 
-    load_qkv.wait()
-    gather.begin(QKV)
+    for kind in QKV:
+        load_qkv[kind].wait()
+        gather.begin(kind)
     load_hidden.wait()
-    load_scales.wait()
+    scales_all[column, 0:1, :] = norm_gain[...].astype(jnp.float32).reshape(1, width)
+    scales_all[column, 1:2, :] = norm_shift[...].astype(jnp.float32).reshape(1, width)
+    scales_all[column, 2:8, :] = jnp.zeros((6, width), jnp.float32)
+    biases[0:1, :] = out_bias[...].astype(jnp.float32).reshape(1, width)
+    for kind in QKV:
+        biases[kind + 1 : kind + 2, :] = qkv_bias[kind : kind + 1, :].astype(jnp.float32)
     send_hidden = beside(inputs.at[column], inputs.at[column], 0)
     send_scales = beside(scales_all.at[column], scales_all.at[column], 1)
     send_hidden.start()
@@ -344,29 +362,39 @@
     scale_factor = 1.0 / math.sqrt(HEAD)
 
     for distance in range(CHIPS_Z):
-        gather.step(QKV, distance)
+        for kind in QKV:
+            gather.step(kind, distance)
     gather.begin(OUT)
-    gather.step(QKV, CHIPS_Z)
-    gather.finish(QKV)
+    for kind in QKV:
+        gather.step(kind, CHIPS_Z)
+    gather.step(OUT, 0)
+    gather.step(OUT, 1)
+    for kind in QKV:
+        gather.finish(kind)
     send_hidden.wait_recv()
     send_scales.wait_recv()
     load_cache.wait()
 
     tile = 512
 
-    def project(layer, source):
-        def one(j, carry):
-            columns = pl.ds(pl.multiple_of(j * tile, tile), tile)
-            total = jnp.dot(
-                source[0], qkv_rows[:width, columns], preferred_element_type=jnp.float32
-            )
-            total += jnp.dot(
-                source[1], qkv_rows[width:, columns], preferred_element_type=jnp.float32
-            )
-            projected[layer, :, columns] = (total + qkv_bias[:, columns]).astype(jnp.bfloat16)
-            return carry
-
-        lax.fori_loop(0, 3 * width // tile, one, 0)
+    def project(layer, source, between):
+        for kind in QKV:
+
+            def one(j, carry, kind=kind):
+                here = pl.ds(pl.multiple_of(j * tile, tile), tile)
+                columns = pl.ds(pl.multiple_of(kind * width + j * tile, tile), tile)
+                total = jnp.dot(
+                    source[0], qkv_rows[:width, columns], preferred_element_type=jnp.float32
+                )
+                total += jnp.dot(
+                    source[1], qkv_rows[width:, columns], preferred_element_type=jnp.float32
+                )
+                total = total + biases[kind + 1 : kind + 2, here]
+                projected[layer, :, columns] = total.astype(jnp.bfloat16)
+                return carry
+
+            lax.fori_loop(0, width // tile, one, 0)
+            between(kind)
         stores = []
         for kind in range(2):
             block = projected.at[layer, :, (kind + 1) * width : (kind + 2) * width]
@@ -377,53 +405,61 @@
             stores.append(store)
         return stores
 
+    contract = (((1,), (1,)), ((), ()))
+    exponent_scale = scale_factor * math.log2(math.e)
+
     def attend_heads(layer, first, count):
-        def one(head, carry):
-            place = head * HEAD
-            here = pl.ds(pl.multiple_of(place, HEAD), HEAD)
-            key_columns = pl.ds(pl.multiple_of(place + width, HEAD), HEAD)
-            value_columns = pl.ds(pl.multiple_of(place + 2 * width, HEAD), HEAD)
-            keys_cached = cache_here[layer, 0, :, here]
-            values_cached = cache_here[layer, 1, :, here]
+        for head in range(first, first + count):
+            here = slice(head * HEAD, (head + 1) * HEAD)
+            key_columns = slice(width + head * HEAD, width + (head + 1) * HEAD)
+            value_columns = slice(2 * width + head * HEAD, 2 * width + (head + 1) * HEAD)
+            scores_all = lax.dot_general(
+                projected[layer, :, here],
+                cache_here[layer, 0, :, here],
+                contract,
+                preferred_element_type=jnp.float32,
+            )
+            weights_all, totals, combined_new = [], [], []
             for request in range(requests):
                 rows = slice(request * SPAN, (request + 1) * SPAN)
-                queries = projected[layer, rows, here]
-                keys_new = projected[layer, rows, key_columns]
-                values_new = projected[layer, rows, value_columns]
-                contract = (((1,), (1,)), ((), ()))
-                scores_cache = lax.dot_general(
-                    queries, keys_cached, contract, preferred_element_type=jnp.float32
+                scores_new = lax.dot_general(
+                    projected[layer, rows, here],
+                    projected[layer, rows, key_columns],
+                    contract,
+                    preferred_element_type=jnp.float32,
                 )
-                scores_new = lax.dot_general(
-                    queries, keys_new, contract, preferred_element_type=jnp.float32
-                )
-                scores_cache = scores_cache * scale_factor + live[request, 0:1, :]
-                scores_new = jnp.where(later, NEGATIVE, scores_new * scale_factor)
+                scores_cache = scores_all[rows, :] + live[request, 0:1, :]
+                scores_new = jnp.where(later, NEGATIVE, scores_new)
                 top = jnp.maximum(
                     jnp.max(scores_cache, axis=1, keepdims=True),
                     jnp.max(scores_new, axis=1, keepdims=True),
                 )
-                weights_cache = jnp.exp(scores_cache - top)
-                weights_new = jnp.exp(scores_new - top)
-                totals = jnp.sum(weights_cache, axis=1, keepdims=True) + jnp.sum(
-                    weights_new, axis=1, keepdims=True
+                weights_cache = jnp.exp2((scores_cache - top) * exponent_scale)
+                weights_new = jnp.exp2((scores_new - top) * exponent_scale)
+                totals.append(
+                    jnp.sum(weights_cache, axis=1, keepdims=True)
+                    + jnp.sum(weights_new, axis=1, keepdims=True)
                 )
-                combined = jnp.dot(
-                    weights_cache.astype(jnp.bfloat16),
-                    values_cached,
-                    preferred_element_type=jnp.float32,
+                weights_all.append(weights_cache.astype(jnp.bfloat16))
+                combined_new.append(
+                    jnp.dot(
+                        weights_new.astype(jnp.bfloat16),
+                        projected[layer, rows, value_columns],
+                        preferred_element_type=jnp.float32,
+                    )
                 )
-                combined += jnp.dot(
-                    weights_new.astype(jnp.bfloat16),
-                    values_new,
-                    preferred_element_type=jnp.float32,
-                )
-                attended[layer, column, rows, here] = (combined / totals).astype(jnp.bfloat16)
-            return carry
-
-        lax.fori_loop(first, first + count, one, 0)
+            combined = jnp.dot(
+                jnp.concatenate(weights_all, axis=0),
+                cache_here[layer, 1, :, here],
+                preferred_element_type=jnp.float32,
+            )
+            combined = (combined + jnp.concatenate(combined_new, axis=0)) / jnp.concatenate(
+                totals, axis=0
+            )
+            attended[layer, column, :, here] = combined.astype(jnp.bfloat16)
 
     group = 2
+    mix_tile = 256
 
     def attend_all(layer, between):
         copies = []
@@ -437,25 +473,31 @@
         return copies
 
     def mix(layer, carried, after):
-        for number in range(width // tile):
-            columns = slice(number * tile, (number + 1) * tile)
+        for number in range(width // mix_tile):
+            columns = slice(number * mix_tile, (number + 1) * mix_tile)
             total = jnp.dot(
                 attended[layer, 0], out_rows[:width, columns], preferred_element_type=jnp.float32
             )
             total += jnp.dot(
                 attended[layer, 1], out_rows[width:, columns], preferred_element_type=jnp.float32
             )
-            total = total + out_bias[:, columns] + carried[column, :, columns].astype(jnp.float32)
+            total = total + biases[0:1, columns] + carried[column, :, columns].astype(jnp.float32)
             summed[layer, column, :, columns] = total.astype(jnp.bfloat16)
             after(number, columns)
 
-    stores = project(0, inputs)
-    gather.step(OUT, 0)
+    def advance_early(kind):
+        if kind == KEY:
+            gather.step(OUT, 2)
 
     def advance(number):
-        gather.step(OUT, number + 1)
-
+        if number == 0:
+            gather.step(OUT, 3)
+        if number == 2:
+            gather.step(OUT, 4)
+
+    stores = project(0, inputs, advance_early)
     copies = attend_all(0, advance)
+    gather.drain()
     gather.finish(OUT)
     for copy in copies:
         copy.wait_recv()
@@ -491,7 +533,7 @@
 
     lax.fori_loop(0, tokens // chunk, norm_rows, 0)
 
-    stores += project(1, normed)
+    stores += project(1, normed, lambda kind: None)
     copies = attend_all(1, lambda number: None)
     for copy in copies:
         copy.wait_recv()
@@ -506,21 +548,25 @@
         mean = jnp.sum(values, axis=1, keepdims=True) / width
         centered = values - mean
         spread = jnp.sum(centered * centered, axis=1, keepdims=True)
-        stats[column, rows, :] = jnp.where(lane == 0, mean, jnp.where(lane == 1, spread, 0.0))
+        stats_wide[0, rows, :] = jnp.where(lane == 0, mean, jnp.where(lane == 1, spread, 0.0))
         return carry
 
     lax.fori_loop(0, tokens // chunk, stat_rows, 0)
-    send_stats = beside(stats.at[column], stats.at[column], 12)
+    stats[column] = jnp.transpose(stats_wide[0])[:8, :]
+    send_stats = beside(stats.at[column], stats.at[column], 14)
     send_stats.start()
     send_stats.wait_recv()
     sides.append(send_stats)
+    for half in range(2):
+        padded = jnp.concatenate([stats[half], jnp.zeros((120, tokens), jnp.float32)], axis=0)
+        stats_wide[half] = jnp.transpose(padded)
 
     def last_rows(j, carry):
         rows = pl.ds(pl.multiple_of(j * chunk, chunk), chunk)
-        mean_a, mean_b = stats[0, rows, 0:1], stats[1, rows, 0:1]
+        mean_a, mean_b = stats_wide[0, rows, 0:1], stats_wide[1, rows, 0:1]
         means = (mean_a + mean_b) * 0.5
         gap = mean_a - mean_b
-        spread = stats[0, rows, 1:2] + stats[1, rows, 1:2] + gap * gap * (width * 0.5)
+        spread = stats_wide[0, rows, 1:2] + stats_wide[1, rows, 1:2] + gap * gap * (width * 0.5)
         inverse = lax.rsqrt(spread / full_width + EPSILON)
         scaled = (summed[1, column, rows, :].astype(jnp.float32) - means) * inverse
         scaled = scaled * scales_all[column, 0:1, :] + scales_all[column, 1:2, :]
@@ -533,7 +579,6 @@
         store.wait()
     for copy in sides:
         copy.wait_send()
-    gather.drain()
 
 
 def fused(
@@ -553,8 +598,6 @@
     shard_rows = w_qkv.shape[0]
     depth = shard_rows * lax.axis_size("wide")
     requests = cache_lengths.shape[0]
-    scales = jnp.stack([norm_gain, norm_shift]).astype(jnp.float32)
-    scales = jnp.concatenate([scales, jnp.zeros((6, width), jnp.float32)])
     smem = pl.BlockSpec(memory_space=pltpu.SMEM)
     vmem = pl.BlockSpec(memory_space=pltpu.VMEM)
     anywhere = pl.BlockSpec(memory_space=pl.ANY)
@@ -565,7 +608,7 @@
             jax.ShapeDtypeStruct((tokens, width), bf16),
             jax.ShapeDtypeStruct((LAYERS, 2, tokens, width), bf16),
         ),
-        in_specs=[smem, smem, anywhere, anywhere, anywhere, anywhere, vmem, vmem, anywhere],
+        in_specs=[smem, smem, anywhere, anywhere, anywhere, anywhere, vmem, vmem, vmem, vmem],
         out_specs=(vmem, anywhere),
         scratch_shapes=[
             pltpu.VMEM((depth, 3 * width), bf16),
@@ -577,13 +620,15 @@
             pltpu.VMEM((LAYERS, 2, tokens, width), bf16),
             pltpu.VMEM((2, tokens, width), bf16),
             pltpu.VMEM((2, 8, width), jnp.float32),
+            pltpu.VMEM((8, width), jnp.float32),
+            pltpu.VMEM((2, 8, tokens), jnp.float32),
             pltpu.VMEM((2, tokens, 128), jnp.float32),
             pltpu.VMEM((requests, 8, cache_count), jnp.float32),
-            pltpu.SemaphoreType.DMA((2, 2, CHIPS_Z * CHIPS_Y, 4)),
-            pltpu.SemaphoreType.DMA((2, 2, CHIPS_Z * CHIPS_Y * CORES)),
-            pltpu.SemaphoreType.DMA((9,)),
-            pltpu.SemaphoreType.DMA((13,)),
-            pltpu.SemaphoreType.DMA((13,)),
+            pltpu.SemaphoreType.DMA((4, 2, CHIPS_Z * CHIPS_Y, 4)),
+            pltpu.SemaphoreType.DMA((4, 2, CHIPS_Z * CHIPS_Y * CORES)),
+            pltpu.SemaphoreType.DMA((12,)),
+            pltpu.SemaphoreType.DMA((15,)),
+            pltpu.SemaphoreType.DMA((15,)),
         ],
         compiler_params=pltpu.CompilerParams(
             collective_id=0, has_side_effects=True, vmem_limit_bytes=VMEM_BYTES
@@ -598,11 +643,12 @@
         cache_offsets,
         hidden_in,
         cache_kv,
-        w_qkv.reshape(shard_rows, 3 * width),
+        jnp.transpose(w_qkv, (1, 0, 2)),
         w_out,
-        qkv_bias.astype(jnp.float32).reshape(1, 3 * width),
-        out_bias.astype(jnp.float32).reshape(1, width),
-        scales,
+        qkv_bias,
+        out_bias,
+        norm_gain,
+        norm_shift,
     )
 
 

time: 161 us -> 148 us (0.919)
  Pallas kernels: 148 us -> 138 us
  other arithmetic: 2.6 us -> 0 us
    pallas_call x1, Pallas kernels: 148 us -> 138 us  [fused(): pl.pallas_call(fused_kernel, out_shape=(jax.ShapeDtypeStruct((tokens, wid...]
    unnamed x4 -> x20, local copies, waits for them, and re-layouts: 7.06 us -> 9.28 us
where the time goes in v2:
time: 148 us
  Pallas kernels  138 us (93%)
  local copies, waits for them, and re-layouts  9.28 us (6%)
    pallas_call x1, Pallas kernels, fused(): pl.pallas_call(fused_kernel, out_shape=(jax.ShapeDtypeStruct((tokens, wid...  138 us
    unnamed x20, local copies, waits for them, and re-layouts  9.28 us

profile of v2, /device:TPU:0, one launch (start us, length us, event | category | flops | bytes accessed | tf_op | source)
XLA Modules:
  0.0 148.1 jit_solution(8316411218890739762)
XLA Ops:
  0.6 0.0 copy-start
  0.6 1.1 copy-done
  1.8 0.0 copy-start.1
  1.8 1.0 copy-done.1
  2.8 0.0 copy-start.2
  2.8 0.9 copy-done.2
  3.8 0.0 copy-start.3
  3.8 0.7 copy-done.3
  4.5 0.0 copy-start.4
  4.5 0.7 copy-done.4
  5.1 0.0 copy-start.5
  5.1 0.7 copy-done.5
  5.8 0.0 copy-start.6
  5.8 0.7 copy-done.6
  6.5 0.0 copy-start.7
  6.5 0.7 copy-done.7
  7.2 0.0 copy-start.8
  7.2 0.7 copy-done.8
  7.8 138.2 %shard_map.113 = (bf16[256,1024]{1,0:T(8,128)(2,1)S(1)}, bf16[2,2,256,1024]{3,2,1,0:T(8,128)(2,1)S(1)}) custom-call(s32[2]{0:T(128)S(1)} %copy-done.7, s32[2]{0:T(128)S(1)} %copy-done.8, bf16[256,1024]{1,0:T(8,128)(2,1)S(1)} %copy-done.1, bf16[2,2,1024,1024]{3,2,1,0:T(8,128)(2,1)} %cache.1, bf16[3,128,1024]{2,1,0:T(8,128)(2,1)S(1)} %bitcast.1, ...), custom_call_target="tpu_custom_call" | custom-call | flops 8589934592 | bytes 16777216 | tf_op jit(solution)/shard_map/pallas_call | solution.py:605
  146.0 0.8 copy.14
  146.8 1.3 copy.15
Async XLA Ops:
  0.6 1.1 copy-start
  1.8 1.0 copy-start.1
  2.8 0.9 copy-start.2
  3.8 0.7 copy-start.3
  4.5 0.7 copy-start.4
  5.1 0.7 copy-start.5
  5.8 0.7 copy-start.6
  6.5 0.7 copy-start.7
  7.2 0.7 copy-start.8

commit v3 on v2

--- a/solution.py
+++ b/solution.py
@@ -251,18 +251,24 @@
 
 
 def fused_kernel(
-    lengths,
-    offsets,
+    lengths_in,
+    offsets_in,
     hidden,
     cache,
     w_qkv,
     w_out,
+    qkv_bias_in,
+    out_bias_in,
+    norm_gain_in,
+    norm_shift_in,
+    hidden_out,
+    new_cache,
+    lengths,
+    offsets,
     qkv_bias,
     out_bias,
     norm_gain,
     norm_shift,
-    hidden_out,
-    new_cache,
     qkv_rows,
     out_rows,
     cache_here,
@@ -315,7 +321,19 @@
     load_out = pltpu.make_async_copy(w_out, out_rows.at[own_rows, :], local_sem.at[1])
     load_hidden = pltpu.make_async_copy(hidden, inputs.at[column], local_sem.at[2])
     load_cache = pltpu.make_async_copy(cache, cache_here, local_sem.at[3])
-    for load in (*load_qkv, load_hidden, load_out, load_cache):
+    pairs = (
+        (lengths_in, lengths),
+        (offsets_in, offsets),
+        (qkv_bias_in, qkv_bias),
+        (out_bias_in, out_bias),
+        (norm_gain_in, norm_gain),
+        (norm_shift_in, norm_shift),
+    )
+    load_small = [
+        pltpu.make_async_copy(source, target, local_sem.at[12 + number])
+        for number, (source, target) in enumerate(pairs)
+    ]
+    for load in (*load_qkv, load_hidden, load_out, *load_small, load_cache):
         load.start()
 
     has_lower = (gather.z + CHIPS_Z - 1) // CHIPS_Z
@@ -336,6 +354,8 @@
         load_qkv[kind].wait()
         gather.begin(kind)
     load_hidden.wait()
+    for load in load_small:
+        load.wait()
     scales_all[column, 0:1, :] = norm_gain[...].astype(jnp.float32).reshape(1, width)
     scales_all[column, 1:2, :] = norm_shift[...].astype(jnp.float32).reshape(1, width)
     scales_all[column, 2:8, :] = jnp.zeros((6, width), jnp.float32)
@@ -377,24 +397,26 @@
 
     tile = 512
 
-    def project(layer, source, between):
+    def project(layer, source, rows, between):
         for kind in QKV:
 
             def one(j, carry, kind=kind):
                 here = pl.ds(pl.multiple_of(j * tile, tile), tile)
                 columns = pl.ds(pl.multiple_of(kind * width + j * tile, tile), tile)
                 total = jnp.dot(
-                    source[0], qkv_rows[:width, columns], preferred_element_type=jnp.float32
+                    source[0, rows, :], qkv_rows[:width, columns], preferred_element_type=jnp.float32
                 )
                 total += jnp.dot(
-                    source[1], qkv_rows[width:, columns], preferred_element_type=jnp.float32
+                    source[1, rows, :], qkv_rows[width:, columns], preferred_element_type=jnp.float32
                 )
                 total = total + biases[kind + 1 : kind + 2, here]
-                projected[layer, :, columns] = total.astype(jnp.bfloat16)
+                projected[layer, rows, columns] = total.astype(jnp.bfloat16)
                 return carry
 
             lax.fori_loop(0, width // tile, one, 0)
             between(kind)
+
+    def store_cache(layer):
         stores = []
         for kind in range(2):
             block = projected.at[layer, :, (kind + 1) * width : (kind + 2) * width]
@@ -408,27 +430,29 @@
     contract = (((1,), (1,)), ((), ()))
     exponent_scale = scale_factor * math.log2(math.e)
 
-    def attend_heads(layer, first, count):
+    def attend_heads(layer, first, count, first_request, last_request):
+        span = slice(first_request * SPAN, last_request * SPAN)
         for head in range(first, first + count):
             here = slice(head * HEAD, (head + 1) * HEAD)
             key_columns = slice(width + head * HEAD, width + (head + 1) * HEAD)
             value_columns = slice(2 * width + head * HEAD, 2 * width + (head + 1) * HEAD)
             scores_all = lax.dot_general(
-                projected[layer, :, here],
+                projected[layer, span, here],
                 cache_here[layer, 0, :, here],
                 contract,
                 preferred_element_type=jnp.float32,
             )
             weights_all, totals, combined_new = [], [], []
-            for request in range(requests):
+            for request in range(first_request, last_request):
                 rows = slice(request * SPAN, (request + 1) * SPAN)
+                within = request - first_request
                 scores_new = lax.dot_general(
                     projected[layer, rows, here],
                     projected[layer, rows, key_columns],
                     contract,
                     preferred_element_type=jnp.float32,
                 )
-                scores_cache = scores_all[rows, :] + live[request, 0:1, :]
+                scores_cache = scores_all[within * SPAN : (within + 1) * SPAN, :] + live[request, 0:1, :]
                 scores_new = jnp.where(later, NEGATIVE, scores_new)
                 top = jnp.maximum(
                     jnp.max(scores_cache, axis=1, keepdims=True),
@@ -456,33 +480,30 @@
             combined = (combined + jnp.concatenate(combined_new, axis=0)) / jnp.concatenate(
                 totals, axis=0
             )
-            attended[layer, column, :, here] = combined.astype(jnp.bfloat16)
-
-    group = 2
-    mix_tile = 256
-
-    def attend_all(layer, between):
-        copies = []
-        for number, first in enumerate(range(0, heads, group)):
-            attend_heads(layer, first, group)
-            block = attended.at[layer, column, :, first * HEAD : (first + group) * HEAD]
-            copy = beside(block, block, 2 + layer * 4 + number)
-            copy.start()
-            copies.append(copy)
-            between(number)
-        return copies
-
-    def mix(layer, carried, after):
-        for number in range(width // mix_tile):
-            columns = slice(number * mix_tile, (number + 1) * mix_tile)
+            attended[layer, column, span, here] = combined.astype(jnp.bfloat16)
+
+    def share_heads(layer, first, count, rows, number):
+        block = attended.at[layer, column, rows, first * HEAD : (first + count) * HEAD]
+        copy = beside(block, block, 2 + layer * 4 + number)
+        copy.start()
+        sides.append(copy)
+        return copy
+
+    def mix(layer, carried, rows, after):
+        for number in range(width // tile):
+            columns = slice(number * tile, (number + 1) * tile)
             total = jnp.dot(
-                attended[layer, 0], out_rows[:width, columns], preferred_element_type=jnp.float32
+                attended[layer, 0, rows, :],
+                out_rows[:width, columns],
+                preferred_element_type=jnp.float32,
             )
             total += jnp.dot(
-                attended[layer, 1], out_rows[width:, columns], preferred_element_type=jnp.float32
+                attended[layer, 1, rows, :],
+                out_rows[width:, columns],
+                preferred_element_type=jnp.float32,
             )
-            total = total + biases[0:1, columns] + carried[column, :, columns].astype(jnp.float32)
-            summed[layer, column, :, columns] = total.astype(jnp.bfloat16)
+            total = total + biases[0:1, columns] + carried[column, rows, columns].astype(jnp.float32)
+            summed[layer, column, rows, columns] = total.astype(jnp.bfloat16)
             after(number, columns)
 
     def advance_early(kind):
@@ -495,26 +516,31 @@
         if number == 2:
             gather.step(OUT, 4)
 
-    stores = project(0, inputs, advance_early)
-    copies = attend_all(0, advance)
+    everything = slice(0, tokens)
+    spans = [slice(request * SPAN, (request + 1) * SPAN) for request in range(requests)]
+    project(0, inputs, everything, advance_early)
+    stores = store_cache(0)
+    group = heads // 4
+    copies = []
+    for number in range(4):
+        attend_heads(0, number * group, group, 0, requests)
+        copies.append(share_heads(0, number * group, group, everything, number))
+        advance(number)
     gather.drain()
     gather.finish(OUT)
     for copy in copies:
         copy.wait_recv()
-    sides += copies
-
-    exchanged = []
-
-    def share(number, columns):
-        block = summed.at[0, column, :, columns]
-        copy = beside(block, block, 10 + number)
-        copy.start()
-        exchanged.append(copy)
-
-    mix(0, inputs, share)
-    for copy in exchanged:
-        copy.wait_recv()
-    sides += exchanged
+
+    exchanged = [[] for _ in spans]
+    for request, rows in enumerate(spans):
+
+        def share(number, columns, request=request, rows=rows):
+            block = summed.at[0, column, rows, columns]
+            copy = beside(block, block, 10 + 2 * request + number)
+            copy.start()
+            exchanged[request].append(copy)
+
+        mix(0, inputs, rows, share)
 
     chunk = 64
 
@@ -531,14 +557,22 @@
             normed[half, rows, :] = scaled.astype(jnp.bfloat16)
         return carry
 
-    lax.fori_loop(0, tokens // chunk, norm_rows, 0)
-
-    stores += project(1, normed, lambda kind: None)
-    copies = attend_all(1, lambda number: None)
-    for copy in copies:
-        copy.wait_recv()
-    sides += copies
-    mix(1, normed, lambda number, columns: None)
+
+    half_heads = heads // 2
+    copies = [[] for _ in spans]
+    chunks = SPAN // chunk
+    for request, rows in enumerate(spans):
+        for copy in exchanged[request]:
+            copy.wait_recv()
+        sides += exchanged[request]
+        lax.fori_loop(request * chunks, (request + 1) * chunks, norm_rows, 0)
+        project(1, normed, rows, lambda kind: None)
+        for number in range(2):
+            attend_heads(1, number * half_heads, half_heads, request, request + 1)
+            copies[request].append(
+                share_heads(1, number * half_heads, half_heads, rows, 2 * request + number)
+            )
+    stores += store_cache(1)
 
     lane = lax.broadcasted_iota(jnp.int32, (chunk, 128), 1)
 
@@ -551,7 +585,11 @@
         stats_wide[0, rows, :] = jnp.where(lane == 0, mean, jnp.where(lane == 1, spread, 0.0))
         return carry
 
-    lax.fori_loop(0, tokens // chunk, stat_rows, 0)
+    for request, rows in enumerate(spans):
+        for copy in copies[request]:
+            copy.wait_recv()
+        mix(1, normed, rows, lambda number, columns: None)
+        lax.fori_loop(request * chunks, (request + 1) * chunks, stat_rows, 0)
     stats[column] = jnp.transpose(stats_wide[0])[:8, :]
     send_stats = beside(stats.at[column], stats.at[column], 14)
     send_stats.start()
@@ -598,8 +636,20 @@
     shard_rows = w_qkv.shape[0]
     depth = shard_rows * lax.axis_size("wide")
     requests = cache_lengths.shape[0]
-    smem = pl.BlockSpec(memory_space=pltpu.SMEM)
     vmem = pl.BlockSpec(memory_space=pltpu.VMEM)
+    hbm = pl.BlockSpec(memory_space=pltpu.HBM)
+    operands = (
+        cache_lengths,
+        cache_offsets,
+        hidden_in,
+        cache_kv,
+        jnp.transpose(w_qkv, (1, 0, 2)),
+        w_out,
+        qkv_bias,
+        out_bias,
+        norm_gain,
+        norm_shift,
+    )
     anywhere = pl.BlockSpec(memory_space=pl.ANY)
     bf16 = jnp.bfloat16
     return pl.pallas_call(
@@ -608,9 +658,15 @@
             jax.ShapeDtypeStruct((tokens, width), bf16),
             jax.ShapeDtypeStruct((LAYERS, 2, tokens, width), bf16),
         ),
-        in_specs=[smem, smem, anywhere, anywhere, anywhere, anywhere, vmem, vmem, vmem, vmem],
+        in_specs=[hbm] * 10,
         out_specs=(vmem, anywhere),
         scratch_shapes=[
+            pltpu.SMEM((requests,), jnp.int32),
+            pltpu.SMEM((requests,), jnp.int32),
+            pltpu.VMEM((3, width), bf16),
+            pltpu.VMEM((width,), bf16),
+            pltpu.VMEM((width,), bf16),
+            pltpu.VMEM((width,), bf16),
             pltpu.VMEM((depth, 3 * width), bf16),
             pltpu.VMEM((depth, width), bf16),
             pltpu.VMEM((LAYERS, 2, cache_count, width), bf16),
@@ -626,7 +682,7 @@
             pltpu.VMEM((requests, 8, cache_count), jnp.float32),
             pltpu.SemaphoreType.DMA((4, 2, CHIPS_Z * CHIPS_Y, 4)),
             pltpu.SemaphoreType.DMA((4, 2, CHIPS_Z * CHIPS_Y * CORES)),
-            pltpu.SemaphoreType.DMA((12,)),
+            pltpu.SemaphoreType.DMA((18,)),
             pltpu.SemaphoreType.DMA((15,)),
             pltpu.SemaphoreType.DMA((15,)),
         ],
@@ -638,18 +694,7 @@
             bytes_accessed=2 * depth * 4 * width,
             transcendentals=LAYERS * tokens * cache_count * (width // HEAD),
         ),
-    )(
-        cache_lengths,
-        cache_offsets,
-        hidden_in,
-        cache_kv,
-        jnp.transpose(w_qkv, (1, 0, 2)),
-        w_out,
-        qkv_bias,
-        out_bias,
-        norm_gain,
-        norm_shift,
-    )
+    )(*(pltpu.with_memory_space_constraint(operand, pltpu.HBM) for operand in operands))
 
 
 def solution(mesh):

time: 148 us -> 137 us (0.926)
  local copies, waits for them, and re-layouts: 9.28 us -> 2.11 us
  Pallas kernels: 138 us -> 134 us
    unnamed x20 -> x2, local copies, waits for them, and re-layouts: 9.28 us -> 2.11 us
    pallas_call x1, Pallas kernels: 138 us -> 134 us  [fused(): pl.pallas_call(fused_kernel, out_shape=(jax.ShapeDtypeStruct((tokens, wid...]
where the time goes in v3:
time: 137 us
  Pallas kernels  134 us (98%)
  local copies, waits for them, and re-layouts  2.11 us (2%)
    pallas_call x1, Pallas kernels, fused(): pl.pallas_call(fused_kernel, out_shape=(jax.ShapeDtypeStruct((tokens, wid...  134 us

profile of v3, /device:TPU:0, one launch (start us, length us, event | category | flops | bytes accessed | tf_op | source)
XLA Modules:
  0.0 137.1 jit_solution(10853942066848097616)
XLA Ops:
  0.6 134.3 %shard_map.113 = (bf16[256,1024]{1,0:T(8,128)(2,1)S(1)}, bf16[2,2,256,1024]{3,2,1,0:T(8,128)(2,1)S(1)}) custom-call(s32[2]{0:T(128)} %lengths_in.1, s32[2]{0:T(128)} %offsets_in.1, bf16[256,1024]{1,0:T(8,128)(2,1)} %hidden.1, bf16[2,2,1024,1024]{3,2,1,0:T(8,128)(2,1)} %cache.1, bf16[3,128,1024]{2,1,0:T(8,128)(2,1)} %bitcast.1, bf16[128,1024]{1,0:T(8,128)(2,1)} %w_out.1, ...), custom_call_target="tpu_custom_call" | custom-call | flops 8589934592 | bytes 16777216 | tf_op jit(solution)/shard_map/pallas_call | solution.py:655
  135.0 0.8 copy.14
  135.8 1.3 copy.15

commit v4 on v3

--- a/solution.py
+++ b/solution.py
@@ -385,20 +385,15 @@
         for kind in QKV:
             gather.step(kind, distance)
     gather.begin(OUT)
-    for kind in QKV:
-        gather.step(kind, CHIPS_Z)
-    gather.step(OUT, 0)
-    gather.step(OUT, 1)
-    for kind in QKV:
-        gather.finish(kind)
     send_hidden.wait_recv()
     send_scales.wait_recv()
     load_cache.wait()
 
     tile = 512
 
-    def project(layer, source, rows, between):
+    def project(layer, source, rows, before):
         for kind in QKV:
+            before(kind)
 
             def one(j, carry, kind=kind):
                 here = pl.ds(pl.multiple_of(j * tile, tile), tile)
@@ -414,7 +409,6 @@
                 return carry
 
             lax.fori_loop(0, width // tile, one, 0)
-            between(kind)
 
     def store_cache(layer):
         stores = []
@@ -429,6 +423,9 @@
 
     contract = (((1,), (1,)), ((), ()))
     exponent_scale = scale_factor * math.log2(math.e)
+
+    def with_ones(values):
+        return jnp.concatenate([values, jnp.ones_like(values)], axis=1)
 
     def attend_heads(layer, first, count, first_request, last_request):
         span = slice(first_request * SPAN, last_request * SPAN)
@@ -442,7 +439,7 @@
                 contract,
                 preferred_element_type=jnp.float32,
             )
-            weights_all, totals, combined_new = [], [], []
+            weights_all, combined_new = [], []
             for request in range(first_request, last_request):
                 rows = slice(request * SPAN, (request + 1) * SPAN)
                 within = request - first_request
@@ -460,26 +457,21 @@
                 )
                 weights_cache = jnp.exp2((scores_cache - top) * exponent_scale)
                 weights_new = jnp.exp2((scores_new - top) * exponent_scale)
-                totals.append(
-                    jnp.sum(weights_cache, axis=1, keepdims=True)
-                    + jnp.sum(weights_new, axis=1, keepdims=True)
-                )
                 weights_all.append(weights_cache.astype(jnp.bfloat16))
                 combined_new.append(
                     jnp.dot(
                         weights_new.astype(jnp.bfloat16),
-                        projected[layer, rows, value_columns],
+                        with_ones(projected[layer, rows, value_columns]),
                         preferred_element_type=jnp.float32,
                     )
                 )
             combined = jnp.dot(
                 jnp.concatenate(weights_all, axis=0),
-                cache_here[layer, 1, :, here],
+                with_ones(cache_here[layer, 1, :, here]),
                 preferred_element_type=jnp.float32,
             )
-            combined = (combined + jnp.concatenate(combined_new, axis=0)) / jnp.concatenate(
-                totals, axis=0
-            )
+            combined = combined + jnp.concatenate(combined_new, axis=0)
+            combined = combined[:, :HEAD] / combined[:, HEAD:]
             attended[layer, column, span, here] = combined.astype(jnp.bfloat16)
 
     def share_heads(layer, first, count, rows, number):
@@ -507,14 +499,14 @@
             after(number, columns)
 
     def advance_early(kind):
-        if kind == KEY:
-            gather.step(OUT, 2)
+        gather.step(kind, CHIPS_Z)
+        gather.finish(kind)
+        if kind == VALUE:
+            gather.step(OUT, 0)
+            gather.step(OUT, 1)
 
     def advance(number):
-        if number == 0:
-            gather.step(OUT, 3)
-        if number == 2:
-            gather.step(OUT, 4)
+        gather.step(OUT, number + 2)
 
     everything = slice(0, tokens)
     spans = [slice(request * SPAN, (request + 1) * SPAN) for request in range(requests)]
@@ -523,10 +515,10 @@
     group = heads // 4
     copies = []
     for number in range(4):
+        if number < 3:
+            advance(number)
         attend_heads(0, number * group, group, 0, requests)
         copies.append(share_heads(0, number * group, group, everything, number))
-        advance(number)
-    gather.drain()
     gather.finish(OUT)
     for copy in copies:
         copy.wait_recv()
@@ -541,6 +533,7 @@
             exchanged[request].append(copy)
 
         mix(0, inputs, rows, share)
+    gather.drain()
 
     chunk = 64
 

time: 137 us -> 135 us (0.985)
  Pallas kernels: 134 us -> 132 us
    pallas_call x1, Pallas kernels: 134 us -> 132 us  [fused(): pl.pallas_call(fused_kernel, out_shape=(jax.ShapeDtypeStruct((tokens, wid...]
where the time goes in v4:
time: 135 us
  Pallas kernels  132 us (98%)
  local copies, waits for them, and re-layouts  2.11 us (2%)
    pallas_call x1, Pallas kernels, fused(): pl.pallas_call(fused_kernel, out_shape=(jax.ShapeDtypeStruct((tokens, wid...  132 us

profile of v4, /device:TPU:0, one launch (start us, length us, event | category | flops | bytes accessed | tf_op | source)
XLA Modules:
  0.0 134.7 jit_solution(11055571284414403382)
XLA Ops:
  0.6 132.0 %shard_map.113 = (bf16[256,1024]{1,0:T(8,128)(2,1)S(1)}, bf16[2,2,256,1024]{3,2,1,0:T(8,128)(2,1)S(1)}) custom-call(s32[2]{0:T(128)} %lengths_in.1, s32[2]{0:T(128)} %offsets_in.1, bf16[256,1024]{1,0:T(8,128)(2,1)} %hidden.1, bf16[2,2,1024,1024]{3,2,1,0:T(8,128)(2,1)} %cache.1, bf16[3,128,1024]{2,1,0:T(8,128)(2,1)} %bitcast.1, bf16[128,1024]{1,0:T(8,128)(2,1)} %w_out.1, ...), custom_call_target="tpu_custom_call" | custom-call | flops 8589934592 | bytes 16777216 | tf_op jit(solution)/shard_map/pallas_call | solution.py:648
  132.6 0.8 copy.14
  133.4 1.3 copy.15

commit v5 on v4

--- a/solution.py
+++ b/solution.py
@@ -203,13 +203,14 @@
         make = functools.partial(self.copy, which, part, z, y, core, SIBLING)
         self.when(valid, lambda: make().wait_recv())
 
-    def begin(self, which):
-        z, y = self.z, self.y
-        self.send(which, SECOND, z, y, (ACROSS,))
-        self.send(which, FIRST, z, y, (UP, DOWN, ACROSS))
-        self.send(which, SECOND, z, y, (UP, DOWN))
-        self.send(which, FIRST, z, y, (SIBLING,))
-        self.send(which, SECOND, z, y, (SIBLING,))
+    def begin_chain(self, which):
+        self.send(which, SECOND, self.z, self.y, (ACROSS,))
+        self.send(which, FIRST, self.z, self.y, (UP, DOWN))
+        self.send(which, SECOND, self.z, self.y, (UP, DOWN))
+
+    def begin_across(self, which):
+        self.send(which, FIRST, self.z, self.y, (ACROSS, SIBLING))
+        self.send(which, SECOND, self.z, self.y, (SIBLING,))
 
     def around(self, distance):
         low, high = self.z - distance, self.z + distance
@@ -352,7 +353,8 @@
 
     for kind in QKV:
         load_qkv[kind].wait()
-        gather.begin(kind)
+        gather.begin_chain(kind)
+        gather.begin_across(kind)
     load_hidden.wait()
     for load in load_small:
         load.wait()
@@ -384,7 +386,9 @@
     for distance in range(CHIPS_Z):
         for kind in QKV:
             gather.step(kind, distance)
-    gather.begin(OUT)
+        if distance == CHIPS_Z - 2:
+            gather.begin_chain(OUT)
+    gather.begin_across(OUT)
     send_hidden.wait_recv()
     send_scales.wait_recv()
     load_cache.wait()
@@ -501,7 +505,7 @@
     def advance_early(kind):
         gather.step(kind, CHIPS_Z)
         gather.finish(kind)
-        if kind == VALUE:
+        if kind == KEY:
             gather.step(OUT, 0)
             gather.step(OUT, 1)
 

time: 135 us -> 132 us (0.978)
  Pallas kernels: 132 us -> 129 us
    pallas_call x1, Pallas kernels: 132 us -> 129 us  [fused(): pl.pallas_call(fused_kernel, out_shape=(jax.ShapeDtypeStruct((tokens, wid...]
where the time goes in v5:
time: 132 us
  Pallas kernels  129 us (98%)
  local copies, waits for them, and re-layouts  2.11 us (2%)
    pallas_call x1, Pallas kernels, fused(): pl.pallas_call(fused_kernel, out_shape=(jax.ShapeDtypeStruct((tokens, wid...  129 us

profile of v5, /device:TPU:0, one launch (start us, length us, event | category | flops | bytes accessed | tf_op | source)
XLA Modules:
  0.0 131.7 jit_solution(13559204607507491202)
XLA Ops:
  0.6 129.0 %shard_map.113 = (bf16[256,1024]{1,0:T(8,128)(2,1)S(1)}, bf16[2,2,256,1024]{3,2,1,0:T(8,128)(2,1)S(1)}) custom-call(s32[2]{0:T(128)} %lengths_in.1, s32[2]{0:T(128)} %offsets_in.1, bf16[256,1024]{1,0:T(8,128)(2,1)} %hidden.1, bf16[2,2,1024,1024]{3,2,1,0:T(8,128)(2,1)} %cache.1, bf16[3,128,1024]{2,1,0:T(8,128)(2,1)} %bitcast.1, bf16[128,1024]{1,0:T(8,128)(2,1)} %w_out.1, ...), custom_call_target="tpu_custom_call" | custom-call | flops 8589934592 | bytes 16777216 | tf_op jit(solution)/shard_map/pallas_call | solution.py:652
  129.6 0.8 copy.14
  130.4 1.3 %copy.15 = bf16[2,2,256,1024]{3,2,1,0:T(8,128)(2,1)} copy(bf16[2,2,256,1024]{3,2,1,0:T(8,128)(2,1)S(1)} %get-tuple-element.5) | data formatting | bytes 4194304
